TPU v7x, 32 devices: a whole 2x2x4 slice. The times are simulated.
32 devices in a mesh: dp: 4 (over z), tensor: 8 (over y, x, core).
Axes of the slice: x: 2, y: 2, z: 4, core: 2. Of those that a mesh axis runs over, the one named last changes fastest.
Arguments:
- activations: bfloat16 [4096, 13312], P('dp', 'tensor'), may hold values from -6 to 6
- plan: int32 [2], replicated, may hold values from 1 to 7, as said below
Outputs:
- covariance_tiles: float32 [2, 1664, 13312], P(None, 'dp', 'tensor')
Inputs may be any that keep to these rules, and one draw needn't show every extreme that they name: `plan`: the masks differ from each other and one of them has every bit of the panel index set.
All inputs are finite; a program needn't handle non-finite values.
Results may differ from a plain program's by a relative error of at most 0.0003.
Values may be sent and summed in bfloat16 or wider, within the bound.
No kernel may reach another device: no remote copies, remote signals or barrier semaphores. Data moves between devices by JAX's collectives and lax.ppermute only.
A program may use at most 128 MiB of HBM per device.

v0:
```python
import math

import jax
import jax.numpy as jnp
from jax import lax
from jax.sharding import PartitionSpec as P

ROUNDS = 2


def swapped(x, axis, apart):
    return lax.ppermute(x, axis, [(i, i ^ 1 << apart) for i in range(lax.axis_size(axis))])


def one_bit(current, mask, bit):
    taken = jnp.bitwise_and(jnp.right_shift(mask, bit), 1) == 1
    received = swapped(current, "tensor", bit)
    return jnp.where(taken, received, current)


def partner_panel(own, mask, width):
    order = list(range(width))
    current = own
    for bit in order:
        current = one_bit(current, mask, bit)
    return current


def shards(activations, plan):
    width = lax.axis_size("tensor").bit_length() - 1
    total_tokens = activations.shape[0] * lax.axis_size("dp")
    scale = jnp.float32(1.0 / math.sqrt(total_tokens))
    tiles = []
    for r in range(ROUNDS):
        other = partner_panel(activations, plan[r], width)
        partial_tile = lax.dot_general(
            other, activations, (((0,), (0,)), ((), ())), preferred_element_type=jnp.float32
        )
        tiles.append(partial_tile)
    stacked = jnp.stack(tiles)
    return lax.psum_scatter(stacked, "dp", scatter_dimension=1, tiled=True) * scale


def solution(mesh):
    return jax.shard_map(
        shards,
        mesh=mesh,
        in_specs=(P("dp", "tensor"), P()),
        out_specs=P(None, "dp", "tensor"),
        check_vma=False,
    )
```

profile of v0, /device:TPU:0, one launch (start us, length us, event | category | flops | bytes accessed | tf_op | source)
XLA Modules:
  0.0 635.6 jit_solution(10634859193740147761)
XLA Ops:
  6.5 0.0 reduce-scatter.2.cloned.1.call-start
  6.5 0.5 collective-permute-start
  7.0 1.3 fusion.4
  9.5 3.4 collective-permute-done
  12.9 2.6 broadcast_select_fusion.2
  15.5 2.9 collective-permute-start.3
  18.4 0.1 collective-permute-start.1
  19.1 73.8 %collective-permute-done.3 = bf16[1024,1664]{1,0:T(8,128)(2,1)S(1)} collective-permute-done((bf16[1024,1664]{1,0:T(8,128)(2,1)S(1)}, bf16[1024,1664]{1,0:T(8,128)(2,1)S(1)}, u32[]{:S(2)}, u32[]{:S(2)}) %collective-permute-start.3) | collective-permute-done | bytes 3407904 | tf_op jit(solution)/shard_map/ppermute | solution.py:12
  92.9 0.4 broadcast_select_fusion.1
  93.3 2.2 collective-permute-start.4
  96.1 69.4 %collective-permute-done.1 = bf16[1024,1664]{1,0:T(8,128)(2,1)S(1)} collective-permute-done((bf16[1024,1664]{1,0:T(8,128)(2,1)S(1)}, bf16[1024,1664]{1,0:T(8,128)(2,1)S(1)}, u32[]{:S(2)}, u32[]{:S(2)}) %collective-permute-start.1) | collective-permute-done | bytes 3407904 | tf_op jit(solution)/shard_map/ppermute | solution.py:12
  165.5 0.0 copy-start
  165.5 0.5 broadcast_select_fusion.3
  166.0 1.8 collective-permute-start.2
  169.1 0.0 collective-permute-done.4
  169.1 0.0 copy-done
  169.1 6.7 %convolution_bitcast_fusion = f32[1,1664,1664]{2,1,0:T(8,128)S(1)} fusion(bf16[1024,1664]{1,0:T(8,128)(2,1)S(1)} %copy-done, bf16[1024,1664]{1,0:T(8,128)(2,1)S(1)} %collective-permute-done.4, bf16[1024,1664]{1,0:T(8,128)(2,1)S(1)} %broadcast_select_fusion.1, pred[]{:T(512)} %bitcast.4), kind=kOutput, calls=%fused_computation.1 | convolution fusion | flops 5672402944 | bytes 21299200 | tf_op jit(solution)/shard_map/dot_general | solution.py:36
  175.7 65.7 %collective-permute-done.2 = bf16[1024,1664]{1,0:T(8,128)(2,1)} collective-permute-done((bf16[1024,1664]{1,0:T(8,128)(2,1)S(1)}, bf16[1024,1664]{1,0:T(8,128)(2,1)}, u32[]{:S(2)}, u32[]{:S(2)}) %collective-permute-start.2) | collective-permute-done | bytes 3407904 | tf_op jit(solution)/shard_map/ppermute | solution.py:12
  241.4 6.8 %convolution_bitcast_fusion.1 = f32[1,1664,1664]{2,1,0:T(8,128)S(1)} fusion(bf16[1024,1664]{1,0:T(8,128)(2,1)S(1)} %copy-done, bf16[1024,1664]{1,0:T(8,128)(2,1)} %collective-permute-done.2, bf16[1024,1664]{1,0:T(8,128)(2,1)S(1)} %broadcast_select_fusion.3, pred[]{:T(512)} %bitcast), kind=kOutput, calls=%fused_computation.2 | convolution fusion | flops 5672402944 | bytes 21299200 | tf_op jit(solution)/shard_map/dot_general | solution.py:36
  248.2 7.8 %pad_maximum_fusion = f32[2,1664,1664]{2,1,0:T(8,128)} fusion(f32[1,1664,1664]{2,1,0:T(8,128)S(1)} %convolution_bitcast_fusion, f32[1,1664,1664]{2,1,0:T(8,128)S(1)} %convolution_bitcast_fusion.1), kind=kLoop, calls=%fused_computation | loop fusion | flops 5537792 | bytes 44302336 | tf_op jit(solution)/shard_map/stack | solution.py:40
  256.0 0.0 reduce-scatter.2.cloned.1.call-update
  256.1 367.3 %reduce-scatter.2.cloned.1.call-done = f32[2,416,1664]{2,1,0:T(8,128)} async-done(((f32[2,1664,1664]{2,1,0:T(8,128)}), f32[2,416,1664]{2,1,0:T(8,128)}) %reduce-scatter.2.cloned.1.call-update) | async-done | bytes 5537808 | tf_op jit(solution)/shard_map/reduce_scatter | solution.py:41
  623.4 5.4 broadcast_multiply_fusion
Async XLA Ops:
  6.5 616.8 %reduce-scatter.2.cloned.1.call-start = ((), (), s32[]{:S(2)}) async-start(), calls=%async_computation.1 | async-start | bytes 27688960 | tf_op jit(solution)/shard_map/reduce_scatter | solution.py:41
  6.5 6.3 collective-permute-start
  15.5 77.4 %collective-permute-start.3 = (bf16[1024,1664]{1,0:T(8,128)(2,1)S(1)}, bf16[1024,1664]{1,0:T(8,128)(2,1)S(1)}, u32[]{:S(2)}, u32[]{:S(2)}) collective-permute-start(bf16[1024,1664]{1,0:T(8,128)(2,1)S(1)} %get-tuple-element.6), channel_id=1, source_target_pairs={{0,2},{1,3},{2,0},{3,1},{4,6},{5,7},{6,4},{7,5},{8,10},{9,11},{10,... | collective-permute-start | bytes 10223624 | tf_op jit(solution)/shard_map/ppermute | solution.py:12
  18.4 147.0 %collective-permute-start.1 = (bf16[1024,1664]{1,0:T(8,128)(2,1)S(1)}, bf16[1024,1664]{1,0:T(8,128)(2,1)S(1)}, u32[]{:S(2)}, u32[]{:S(2)}) collective-permute-start(bf16[1024,1664]{1,0:T(8,128)(2,1)S(1)} %get-tuple-element.5), channel_id=1, source_target_pairs={{0,2},{1,3},{2,0},{3,1},{4,6},{5,7},{6,4},{7,5},{8,10},{9,11},{10,... | collective-permute-start | bytes 10223624 | tf_op jit(solution)/shard_map/ppermute | solution.py:12
  93.3 75.7 %collective-permute-start.4 = (bf16[1024,1664]{1,0:T(8,128)(2,1)S(1)}, bf16[1024,1664]{1,0:T(8,128)(2,1)S(1)}, u32[]{:S(2)}, u32[]{:S(2)}) collective-permute-start(bf16[1024,1664]{1,0:T(8,128)(2,1)S(1)} %broadcast_select_fusion.1), channel_id=1, source_target_pairs={{0,4},{1,5},{2,6},{3,7},{4,0},{5,1},{6,2},{7,3},{8,12},{9,13},{10,... | collective-permute-start | bytes 10223624 | tf_op jit(solution)/shard_map/ppermute | solution.py:12
  165.5 3.6 copy-start
  166.0 75.4 %collective-permute-start.2 = (bf16[1024,1664]{1,0:T(8,128)(2,1)S(1)}, bf16[1024,1664]{1,0:T(8,128)(2,1)}, u32[]{:S(2)}, u32[]{:S(2)}) collective-permute-start(bf16[1024,1664]{1,0:T(8,128)(2,1)S(1)} %broadcast_select_fusion.3), channel_id=1, source_target_pairs={{0,4},{1,5},{2,6},{3,7},{4,0},{5,1},{6,2},{7,3},{8,12},{9,13},{10,... | collective-permute-start | bytes 10223624 | tf_op jit(solution)/shard_map/ppermute | solution.py:12
Sparse Core Ops, SparseCore 0:
  256.2 367.1 reduce-scatter.1
where the time goes:
time: 637 us; the launch traced here: 636 us
  waiting for transfers between devices  580 us (91%)
  between operations  17.1 us (3%)
  other arithmetic  16.7 us (3%)
  matrix products  13.4 us (2%)
  starting transfers between devices  7.44 us (1%)
    reduce_scatter x1, waiting for transfers between devices, shards(): lax.psum_scatter(stacked, 'dp', scatter_dimension=1, tiled=True) * scale  367 us
    ppermute x5, waiting for transfers between devices, swapped(): lax.ppermute(x, axis, [(i, i ^ 1 << apart) for i in range(lax.axis_size(a...  212 us
    dot_general x2, matrix products, shards(): lax.dot_general(other, activations, (((0,), (0,)), ((), ())), preferred_e...  13.4 us
  transfers between devices with their start and end apart: 6, of which 5 were waited for; matrix products, arithmetic and copies ran while one was open for 1% of the time, Pallas kernels for 0%

commit v1 on v0

v1 whole, which is shorter than its diff:
```python
import math

import jax
import jax.numpy as jnp
from jax import lax
from jax.sharding import PartitionSpec as P

ROUNDS = 2
LINE = 4


def swapped(x, axis, apart):
    return lax.ppermute(x, axis, [(i, i ^ 1 << apart) for i in range(lax.axis_size(axis))])


def partner_panel(own, mask, width):
    current = own
    for bit in range(width):
        taken = jnp.bitwise_and(jnp.right_shift(mask, bit), 1) == 1
        current = jnp.where(taken, swapped(current, "tensor", bit), current)
    return current


def shards_any(activations, plan):
    width = lax.axis_size("tensor").bit_length() - 1
    scale = jnp.float32(1.0 / math.sqrt(activations.shape[0] * lax.axis_size("dp")))
    tiles = []
    for r in range(ROUNDS):
        other = partner_panel(activations, plan[r], width)
        tiles.append(
            lax.dot_general(other, activations, (((0,), (0,)), ((), ())), preferred_element_type=jnp.float32)
        )
    return lax.psum_scatter(jnp.stack(tiles), "dp", scatter_dimension=1, tiled=True) * scale


def inward(x):
    return lax.ppermute(x, "dp", [(0, 1), (3, 2)])


def across(x):
    return lax.ppermute(x, "dp", [(1, 2), (2, 1)])


def outward(x):
    return lax.ppermute(x, "dp", [(1, 0), (2, 3)])


def partner(x, mask):
    return lax.ppermute(x, "tensor", [(i, i ^ mask) for i in range(lax.axis_size("tensor"))])


def product(rows, columns):
    return lax.dot_general(rows, columns, (((1,), (1,)), ((), ())), preferred_element_type=jnp.float32)


def packed(tile):
    biggest = jnp.max(jnp.abs(tile))
    power = jnp.ceil(jnp.log2(jnp.maximum(biggest, 1e-30)))
    flat = (tile * jnp.exp2(14.0 - power)).reshape(-1, tile.shape[-1])
    return jnp.concatenate([flat, jnp.full((16, flat.shape[1]), power)]).astype(jnp.float16)


def unpacked(flat, shape):
    power = flat[-1, 0].astype(jnp.float32)
    return flat[:-16].reshape(shape).astype(jnp.float32) * jnp.exp2(power - 14.0)


def line_branch(mask, top):
    rest = top ^ mask

    def run(w0, w1, w2, w3, scale):
        w = [w0, w1, w2, w3]
        e, f, g = [None] * 4, [None] * 4, [None] * 4
        e[3] = inward(w[3])
        f[0] = across(w[3])
        wm = [partner(w[0], mask), None]
        e[2] = inward(w[2])
        g[0] = across(e[3])
        w7 = [partner(wm[0], rest), None]
        em = [inward(wm[0]), None]
        f[1] = across(w[2])
        fm = [partner(f[0], mask), None]
        e7 = [inward(w7[0]), None]
        g[1] = across(e[2])
        gm = [partner(g[0], mask), None]
        f7 = [partner(fm[0], rest), None]
        e[1] = inward(w[1])
        f[2] = across(w[1])
        wm[1] = partner(w[1], mask)
        g7 = [partner(gm[0], rest), None]
        e[0] = inward(w[0])
        g[2] = across(e[1])
        w7[1] = partner(wm[1], rest)
        em[1] = inward(wm[1])
        f[3] = across(w[0])
        fm[1] = partner(f[1], mask)
        e7[1] = inward(w7[1])
        g[3] = across(e[0])
        gm[1] = partner(g[1], mask)
        f7[1] = partner(fm[1], rest)
        g7[1] = partner(gm[1], rest)

        rows_m = [jnp.concatenate([wm[q], em[q], fm[q], gm[q]], 1) for q in range(2)]
        rows_7 = [jnp.concatenate([w7[q], e7[q], f7[q], g7[q]], 1) for q in range(2)]
        columns = [jnp.concatenate([w[j], e[j], f[j], g[j]], 1) for j in range(4)]

        pieces = []
        for j in range(4):
            sent = jnp.stack([product(rows_m[0], columns[j]), product(rows_7[0], columns[j])]) * scale
            pieces.append((sent.shape, outward(packed(sent))))
        middle = (lax.axis_index("dp") == 1) | (lax.axis_index("dp") == 2)
        done = []
        for j in range(4):
            own = jnp.stack([product(rows_m[1], columns[j]), product(rows_7[1], columns[j])]) * scale
            shape, flat = pieces[j]
            done.append(jnp.where(middle, own, unpacked(flat, shape)))
        low = lax.axis_index("dp") < 2
        return [jnp.where(low, done[j], done[3 - j]) for j in range(4)]

    return run


def shards_line(activations, plan):
    tokens, units = activations.shape
    top = lax.axis_size("tensor") - 1
    scale = jnp.float32(1.0 / math.sqrt(tokens * LINE))
    blocks = activations.T.reshape(LINE, units // LINE, tokens)
    low = lax.axis_index("dp") < 2
    w = [jnp.where(low, blocks[j], blocks[3 - j]) for j in range(4)]
    first_is_top = plan[0] == top
    other = plan[0] + plan[1] - top
    pieces = lax.switch(other - 1, [line_branch(m, top) for m in range(1, top)], *w, scale)
    out = jnp.concatenate(pieces, 2)
    return jnp.where(first_is_top, out[::-1], out)


def solution(mesh):
    fast = mesh.shape["dp"] == LINE
    return jax.shard_map(
        shards_line if fast else shards_any,
        mesh=mesh,
        in_specs=(P("dp", "tensor"), P()),
        out_specs=P(None, "dp", "tensor"),
        check_vma=False,
    )
```

time: 637 us -> 392 us (0.62)
  waiting for transfers between devices: 580 us -> 116 us
  local copies, waits for them, and re-layouts: 1.29 us -> 71.7 us
  starting transfers between devices: 7.44 us -> 72.9 us
  matrix products: 13.4 us -> 51 us
  loops' own time: 0 us -> 29.8 us
  other arithmetic: 16.7 us -> 40.8 us
  between operations: 17.1 us -> 2.24 us
    reduce_scatter x1 -> x0, waiting for transfers between devices: 367 us -> none  [shards(): lax.psum_scatter(stacked, 'dp', scatter_dimension=1, tiled=True) * scale]
    ppermute x5 -> x32, waiting for transfers between devices: 212 us -> 116 us  [the longest x8 62.6 us: inward(): return lax.ppermute(x, 'dp', [(0, 1), (3, 2)])]
    ppermute x5 -> x32, starting transfers between devices: 7.44 us -> 72.9 us  [the longest x8 48.4 us: inward(): return lax.ppermute(x, 'dp', [(0, 1), (3, 2)])]
    dot_general x2 -> x16, matrix products: 13.4 us -> 51 us  [product(): lax.dot_general(rows, columns, (((1,), (1,)), ((), ())), preferred_elemen...]
    another operation x0 -> x1, loops' own time: none -> 29.8 us  [shards_line(): lax.switch(other - 1, [line_branch(m, top) for m in range(1, top)], *w, s...]
    cond x0 -> x96, local copies, waits for them, and re-layouts: none -> 26 us
    select_n x3 -> x7, other arithmetic: 3.52 us -> 25.2 us  [the longest x4 9.61 us: run(): done.append(jnp.where(middle, own, unpacked(flat, shape)))]
    concatenate x0 -> x13, local copies, waits for them, and re-layouts: none -> 18.1 us  [the longest x1 7.81 us: shards_line(): out = jnp.concatenate(pieces, 2)]
  transfers between devices with their start and end apart: 6 -> 32, of which waited for: 5 -> 13; matrix products, arithmetic and copies ran while one was open for 1% -> 22% of each run, Pallas kernels for 0% -> 0%
where the time goes in v1:
time: 392 us; the launch traced here: 384 us
  waiting for transfers between devices  116 us (30%)
  starting transfers between devices  72.9 us (19%)
  local copies, waits for them, and re-layouts  71.7 us (18%)
  matrix products  51 us (13%)
  other arithmetic  40.8 us (10%)
  loops' own time  29.8 us (8%)
    ppermute x8, waiting for transfers between devices, inward(): return lax.ppermute(x, 'dp', [(0, 1), (3, 2)])  62.6 us
    dot_general x16, matrix products, product(): lax.dot_general(rows, columns, (((1,), (1,)), ((), ())), preferred_elemen...  51 us
    ppermute x8, starting transfers between devices, inward(): return lax.ppermute(x, 'dp', [(0, 1), (3, 2)])  48.4 us
    another operation x1, loops' own time, shards_line(): lax.switch(other - 1, [line_branch(m, top) for m in range(1, top)], *w, s...  29.8 us
    ppermute x12, waiting for transfers between devices, partner(): lax.ppermute(x, 'tensor', [(i, i ^ mask) for i in range(lax.axis_size('te...  27.5 us
    cond x96, local copies, waits for them, and re-layouts  26 us
    ppermute x4, waiting for transfers between devices, outward(): return lax.ppermute(x, 'dp', [(1, 0), (2, 3)])  25.9 us
    ppermute x12, starting transfers between devices, partner(): lax.ppermute(x, 'tensor', [(i, i ^ mask) for i in range(lax.axis_size('te...  11.7 us
  transfers between devices with their start and end apart: 32, of which 13 were waited for; matrix products, arithmetic and copies ran while one was open for 22% of the time, Pallas kernels for 0%

profile of v1, /device:TPU:0, one launch (start us, length us, event | category | flops | bytes accessed | tf_op | source)
XLA Modules:
  0.0 384.3 jit_solution(12571441691996082480)
XLA Ops:
  0.0 5.6 %copy.52 = bf16[1024,1664]{0,1:T(8,128)(2,1)} copy(bf16[1024,1664]{1,0:T(8,128)(2,1)} %param.8) | data formatting | bytes 6815744 | tf_op args[0]
  9.6 349.6 %conditional.1 = (pred[2,416,416]{2,1,0:T(8,128)(4,1)S(1)}, pred[2,416,416]{2,1,0:T(8,128)(4,1)S(1)}, f32[2,416,416]{2,1,0:T(8,128)}, f32[2,416,416]{2,1,0:T(8,1...) conditional(s32[]{:T(128)} %bitcast.169, ...), branch_computations={%region_0.5_spmd, %region_5.10_spmd, %region_10.15_spmd, %region_1... | conditional | flops 22699409408 | bytes 633333952 | solution.py:132
  10.8 7.3 %collective-permute-start.9 = (bf16[416,1024]{1,0:T(8,128)(2,1)S(1)}, bf16[416,1024]{1,0:T(8,128)(2,1)S(1)}, u32[]{:S(2)}, u32[]{:S(2)}) collective-permute-start(bf16[416,1024]{1,0:T(8,128)(2,1)S(1)} %get-tuple-element.66), channel_id=1, source_target_pairs={{0,8},{24,16},{1,9},{25,17},{2,10},{26,18},{3,11},{27,19},{4,12},{... | collective-permute-start | bytes 2555912 | tf_op jit(solution)/shard_map/cond/branch_0_fun/ppermute | solution.py:37
  20.4 18.8 %collective-permute-start.27 = (bf16[416,1024]{1,0:T(8,128)(2,1)S(1)}, bf16[416,1024]{1,0:T(8,128)(2,1)}, u32[]{:S(2)}, u32[]{:S(2)}) collective-permute-start(bf16[416,1024]{1,0:T(8,128)(2,1)S(1)} %get-tuple-element.63), channel_id=1, source_target_pairs={{0,8},{24,16},{1,9},{25,17},{2,10},{26,18},{3,11},{27,19},{4,12},{... | collective-permute-start | bytes 2555912 | tf_op jit(solution)/shard_map/cond/branch_0_fun/ppermute | solution.py:37
  40.8 14.9 %collective-permute-done.4 = bf16[416,1024]{1,0:T(8,128)(2,1)S(1)} collective-permute-done((bf16[416,1024]{1,0:T(8,128)(2,1)S(1)}, bf16[416,1024]{1,0:T(8,128)(2,1)S(1)}, u32[]{:S(2)}, u32[]{:S(2)}) %collective-permute-start.4) | collective-permute-done | bytes 852000 | tf_op jit(solution)/shard_map/cond/branch_0_fun/ppermute | solution.py:37
  55.7 5.3 %collective-permute-start.7 = (bf16[416,1024]{1,0:T(8,128)(2,1)S(1)}, bf16[416,1024]{1,0:T(8,128)(2,1)}, u32[]{:S(2)}, u32[]{:S(2)}) collective-permute-start(bf16[416,1024]{1,0:T(8,128)(2,1)S(1)} %get-tuple-element.65), channel_id=1, source_target_pairs={{0,8},{24,16},{1,9},{25,17},{2,10},{26,18},{3,11},{27,19},{4,12},{... | collective-permute-start | bytes 2555912 | tf_op jit(solution)/shard_map/cond/branch_0_fun/ppermute | solution.py:37
  78.3 13.2 %collective-permute-done.7 = bf16[416,1024]{1,0:T(8,128)(2,1)} collective-permute-done((bf16[416,1024]{1,0:T(8,128)(2,1)S(1)}, bf16[416,1024]{1,0:T(8,128)(2,1)}, u32[]{:S(2)}, u32[]{:S(2)}) %collective-permute-start.7) | collective-permute-done | bytes 852000 | tf_op jit(solution)/shard_map/cond/branch_0_fun/ppermute | solution.py:37
  97.8 6.3 %collective-permute-start.16 = (bf16[416,1024]{1,0:T(8,128)(2,1)}, bf16[416,1024]{1,0:T(8,128)(2,1)S(1)}, u32[]{:S(2)}, u32[]{:S(2)}) collective-permute-start(bf16[416,1024]{1,0:T(8,128)(2,1)} %collective-permute-done.15), channel_id=1, source_target_pairs={{0,8},{24,16},{1,9},{25,17},{2,10},{26,18},{3,11},{27,19},{4,12},{... | collective-permute-start | bytes 2555912 | tf_op jit(solution)/shard_map/cond/branch_0_fun/ppermute | solution.py:37
  109.7 2.9 collective-permute-done.11
  114.2 9.6 %collective-permute-done.16 = bf16[416,1024]{1,0:T(8,128)(2,1)S(1)} collective-permute-done((bf16[416,1024]{1,0:T(8,128)(2,1)}, bf16[416,1024]{1,0:T(8,128)(2,1)S(1)}, u32[]{:S(2)}, u32[]{:S(2)}) %collective-permute-start.16) | collective-permute-done | bytes 852000 | tf_op jit(solution)/shard_map/cond/branch_0_fun/ppermute | solution.py:37
  124.0 15.7 %collective-permute-done.1 = bf16[416,1024]{1,0:T(8,128)(2,1)S(1)} collective-permute-done((bf16[416,1024]{1,0:T(8,128)(2,1)S(1)}, bf16[416,1024]{1,0:T(8,128)(2,1)S(1)}, u32[]{:S(2)}, u32[]{:S(2)}) %collective-permute-start.1) | collective-permute-done | bytes 852000 | tf_op jit(solution)/shard_map/cond/branch_0_fun/ppermute | solution.py:37
  139.7 4.4 %collective-permute-start.20 = (bf16[416,1024]{1,0:T(8,128)(2,1)}, bf16[416,1024]{1,0:T(8,128)(2,1)S(1)}, u32[]{:S(2)}, u32[]{:S(2)}) collective-permute-start(bf16[416,1024]{1,0:T(8,128)(2,1)} %collective-permute-done.19), channel_id=1, source_target_pairs={{0,8},{24,16},{1,9},{25,17},{2,10},{26,18},{3,11},{27,19},{4,12},{... | collective-permute-start | bytes 2555912 | tf_op jit(solution)/shard_map/cond/branch_0_fun/ppermute | solution.py:37
  144.9 3.5 collective-permute-start.12
  154.4 2.9 convolution_bitcast_fusion.3
  159.3 2.9 convolution_bitcast_fusion.7
  172.1 6.8 %collective-permute-done.12 = bf16[416,1024]{1,0:T(8,128)(2,1)S(1)} collective-permute-done((bf16[416,1024]{1,0:T(8,128)(2,1)S(1)}, bf16[416,1024]{1,0:T(8,128)(2,1)S(1)}, u32[]{:S(2)}, u32[]{:S(2)}) %collective-permute-start.12) | collective-permute-done | bytes 852000 | tf_op jit(solution)/shard_map/cond/branch_0_fun/ppermute | solution.py:37
  178.9 6.5 %collective-permute-done.13 = bf16[416,1024]{1,0:T(8,128)(2,1)S(1)} collective-permute-done((bf16[416,1024]{1,0:T(8,128)(2,1)S(1)}, bf16[416,1024]{1,0:T(8,128)(2,1)S(1)}, u32[]{:S(2)}, u32[]{:S(2)}) %collective-permute-start.13) | collective-permute-done | bytes 852000 | tf_op jit(solution)/shard_map/cond/branch_0_fun/ppermute | solution.py:49
  185.5 2.9 convolution_bitcast_fusion.15
  188.3 15.3 %collective-permute-done.22 = bf16[416,1024]{1,0:T(8,128)(2,1)S(1)} collective-permute-done((bf16[416,1024]{1,0:T(8,128)(2,1)S(1)}, bf16[416,1024]{1,0:T(8,128)(2,1)S(1)}, u32[]{:S(2)}, u32[]{:S(2)}) %collective-permute-start.22) | collective-permute-done | bytes 852000 | tf_op jit(solution)/shard_map/cond/branch_0_fun/ppermute | solution.py:49
  208.4 4.9 %convolution_bitcast_fusion.4 = f32[1,416,416]{2,1,0:T(8,128)S(1)} fusion(bf16[416,4096]{1,0:T(8,128)(2,1)} %copy-done.131, bf16[416,4096]{1,0:T(8,128)(2,1)} %copy-done.162), kind=kOutput, calls=%fused_computation.28 | convolution fusion | flops 1417674752 | bytes 7507968 | tf_op jit(solution)/shard_map/cond/branch_0_fun/dot_general | solution.py:53
  220.8 6.0 %convolution_bitcast_fusion.2 = f32[1,416,416]{2,1,0:T(8,128)} fusion(bf16[416,4096]{1,0:T(8,128)(2,1)} %constant_dynamic-update-slice_fusion.8, bf16[416,4096]{1,0:T(8,128)(2,1)} %copy-done.150), kind=kOutput, calls=%fused_computation.26 | convolution fusion | flops 1417674752 | bytes 7507968 | tf_op jit(solution)/shard_map/cond/branch_0_fun/dot_general | solution.py:53
  226.8 2.9 convolution_bitcast_fusion.6
  234.3 6.0 %convolution_bitcast_fusion.10 = f32[1,416,416]{2,1,0:T(8,128)} fusion(bf16[416,4096]{1,0:T(8,128)(2,1)} %constant_dynamic-update-slice_fusion.8, bf16[416,4096]{1,0:T(8,128)(2,1)} %copy-done.198), kind=kOutput, calls=%fused_computation.34 | convolution fusion | flops 1417674752 | bytes 7507968 | tf_op jit(solution)/shard_map/cond/branch_0_fun/dot_general | solution.py:53
  269.5 5.9 %convolution_bitcast_fusion.14 = f32[1,416,416]{2,1,0:T(8,128)} fusion(bf16[416,4096]{1,0:T(8,128)(2,1)} %constant_dynamic-update-slice_fusion.8, bf16[416,4096]{1,0:T(8,128)(2,1)} %copy-done.180), kind=kOutput, calls=%fused_computation.38 | convolution fusion | flops 1417674752 | bytes 7507968 | tf_op jit(solution)/shard_map/cond/branch_0_fun/dot_general | solution.py:53
  277.4 13.6 %collective-permute-done.28 = f16[848,416]{0,1:T(8,128)(2,1)} collective-permute-done((f16[848,416]{0,1:T(8,128)(2,1)}, f16[848,416]{0,1:T(8,128)(2,1)}, u32[]{:S(2)}, u32[]{:S(2)}) %collective-permute-start.28) | collective-permute-done | bytes 705568 | tf_op jit(solution)/shard_map/cond/branch_0_fun/ppermute | solution.py:45
  299.3 3.1 fusion.3
  304.1 2.9 collective-permute-done.26
  312.7 9.3 %collective-permute-done.23 = f16[848,416]{0,1:T(8,128)(2,1)} collective-permute-done((f16[848,416]{0,1:T(8,128)(2,1)}, f16[848,416]{0,1:T(8,128)(2,1)}, u32[]{:S(2)}, u32[]{:S(2)}) %collective-permute-start.23) | collective-permute-done | bytes 705568 | tf_op jit(solution)/shard_map/cond/branch_0_fun/ppermute | solution.py:45
  328.3 3.0 fusion
  362.2 6.2 %fusion.24 = (f32[2,416,416]{2,1,0:T(8,128)S(1)}, f32[2,416,416]{2,1,0:T(8,128)S(1)}, f32[2,416,416]{2,1,0:T(8,128)}, f32[2,416,416]{2,1,0:T(8,128)}) fusion(pred[2,416,416]{2,1,0:T(8,128)(4,1)} %copy-done.52, f32[2,416,416]{2,1,0:T(8,128)} %copy-done.7, f32[2,416,416]{2,1,0:T(8,128)} %copy-done.6, f32[2,416,416]{2,1,0:T(8,128)} %copy-done.8, ...), kind=kLoop, calls=%fused_computation.437 | loop fusion | flops 1384448 | bytes 11421696 | tf_op jit(solution)/shard_map/cond/branch_0_fun/jit(_where)/select_n | solution.py:118
  368.3 7.8 %concatenate.219 = f32[2,416,1664]{2,1,0:T(8,128)} concatenate(f32[2,416,416]{2,1,0:T(8,128)S(1)} %get-tuple-element.122, f32[2,416,416]{2,1,0:T(8,128)} %get-tuple-element.131, f32[2,416,416]{2,1,0:T(8,128)} %get-tuple-element.132, f32[2,416,416]{2,1,0:T(8,128)S(1)} %get-tuple-element.121), dimensions={2} | concatenate | bytes 11075584 | tf_op jit(solution)/shard_map/concatenate | solution.py:133
  376.8 7.3 %reverse_select_fusion = f32[2,416,1664]{2,1,0:T(8,128)} fusion(f32[2,416,1664]{2,1,0:T(8,128)} %concatenate.219, pred[]{:T(512)} %bitcast.168), kind=kLoop, calls=%fused_computation.432 | loop fusion | flops 1384448 | bytes 11075585 | tf_op jit(solution)/shard_map/jit(_where)/select_n | solution.py:134
  (205 shorter events, 128.7 us)
Async XLA Ops:
  9.6 10.6 %collective-permute-start.15 = (bf16[416,1024]{1,0:T(8,128)(2,1)S(1)}, bf16[416,1024]{1,0:T(8,128)(2,1)}, u32[]{:S(2)}, u32[]{:S(2)}) collective-permute-start(bf16[416,1024]{1,0:T(8,128)(2,1)S(1)} %get-tuple-element.65), channel_id=1, source_target_pairs={{0,1},{1,0},{2,3},{3,2},{4,5},{5,4},{6,7},{7,6},{8,9},{9,8},{10,11... | collective-permute-start | bytes 2555912 | tf_op jit(solution)/shard_map/cond/branch_0_fun/ppermute | solution.py:49
  10.1 10.2 %collective-permute-start.8 = (bf16[416,1024]{1,0:T(8,128)(2,1)S(1)}, bf16[416,1024]{1,0:T(8,128)(2,1)S(1)}, u32[]{:S(2)}, u32[]{:S(2)}) collective-permute-start(bf16[416,1024]{1,0:T(8,128)(2,1)S(1)} %get-tuple-element.66), channel_id=1, source_target_pairs={{8,16},{16,8},{9,17},{17,9},{10,18},{18,10},{11,19},{19,11},{12,20... | collective-permute-start | bytes 2555912 | tf_op jit(solution)/shard_map/cond/branch_0_fun/ppermute | solution.py:41
  10.8 28.4 %collective-permute-start.9 = (bf16[416,1024]{1,0:T(8,128)(2,1)S(1)}, bf16[416,1024]{1,0:T(8,128)(2,1)S(1)}, u32[]{:S(2)}, u32[]{:S(2)}) collective-permute-start(bf16[416,1024]{1,0:T(8,128)(2,1)S(1)} %get-tuple-element.66), channel_id=1, source_target_pairs={{0,8},{24,16},{1,9},{25,17},{2,10},{26,18},{3,11},{27,19},{4,12},{... | collective-permute-start | bytes 2555912 | tf_op jit(solution)/shard_map/cond/branch_0_fun/ppermute | solution.py:37
  18.2 37.5 %collective-permute-start.4 = (bf16[416,1024]{1,0:T(8,128)(2,1)S(1)}, bf16[416,1024]{1,0:T(8,128)(2,1)S(1)}, u32[]{:S(2)}, u32[]{:S(2)}) collective-permute-start(bf16[416,1024]{1,0:T(8,128)(2,1)S(1)} %get-tuple-element.64), channel_id=1, source_target_pairs={{0,8},{24,16},{1,9},{25,17},{2,10},{26,18},{3,11},{27,19},{4,12},{... | collective-permute-start | bytes 2555912 | tf_op jit(solution)/shard_map/cond/branch_0_fun/ppermute | solution.py:37
  19.5 41.5 %collective-permute-start.29 = (bf16[416,1024]{1,0:T(8,128)(2,1)S(1)}, bf16[416,1024]{1,0:T(8,128)(2,1)S(1)}, u32[]{:S(2)}, u32[]{:S(2)}) collective-permute-start(bf16[416,1024]{1,0:T(8,128)(2,1)S(1)} %get-tuple-element.63), channel_id=1, source_target_pairs={{8,16},{16,8},{9,17},{17,9},{10,18},{18,10},{11,19},{19,11},{12,20... | collective-permute-start | bytes 2555912 | tf_op jit(solution)/shard_map/cond/branch_0_fun/ppermute | solution.py:41
  20.3 44.6 %collective-permute-start = (bf16[416,1024]{1,0:T(8,128)(2,1)S(1)}, bf16[416,1024]{1,0:T(8,128)(2,1)S(1)}, u32[]{:S(2)}, u32[]{:S(2)}) collective-permute-start(bf16[416,1024]{1,0:T(8,128)(2,1)S(1)} %get-tuple-element.63), channel_id=1, source_target_pairs={{0,1},{1,0},{2,3},{3,2},{4,5},{5,4},{6,7},{7,6},{8,9},{9,8},{10,11... | collective-permute-start | bytes 2555912 | tf_op jit(solution)/shard_map/cond/branch_0_fun/ppermute | solution.py:49
  20.4 53.6 %collective-permute-start.27 = (bf16[416,1024]{1,0:T(8,128)(2,1)S(1)}, bf16[416,1024]{1,0:T(8,128)(2,1)}, u32[]{:S(2)}, u32[]{:S(2)}) collective-permute-start(bf16[416,1024]{1,0:T(8,128)(2,1)S(1)} %get-tuple-element.63), channel_id=1, source_target_pairs={{0,8},{24,16},{1,9},{25,17},{2,10},{26,18},{3,11},{27,19},{4,12},{... | collective-permute-start | bytes 2555912 | tf_op jit(solution)/shard_map/cond/branch_0_fun/ppermute | solution.py:37
  39.2 37.0 %collective-permute-start.2 = (bf16[416,1024]{1,0:T(8,128)(2,1)S(1)}, bf16[416,1024]{1,0:T(8,128)(2,1)}, u32[]{:S(2)}, u32[]{:S(2)}) collective-permute-start(bf16[416,1024]{1,0:T(8,128)(2,1)S(1)} %get-tuple-element.64), channel_id=1, source_target_pairs={{8,16},{16,8},{9,17},{17,9},{10,18},{18,10},{11,19},{19,11},{12,20... | collective-permute-start | bytes 2555912 | tf_op jit(solution)/shard_map/cond/branch_0_fun/ppermute | solution.py:41
  55.7 35.8 %collective-permute-start.7 = (bf16[416,1024]{1,0:T(8,128)(2,1)S(1)}, bf16[416,1024]{1,0:T(8,128)(2,1)}, u32[]{:S(2)}, u32[]{:S(2)}) collective-permute-start(bf16[416,1024]{1,0:T(8,128)(2,1)S(1)} %get-tuple-element.65), channel_id=1, source_target_pairs={{0,8},{24,16},{1,9},{25,17},{2,10},{26,18},{3,11},{27,19},{4,12},{... | collective-permute-start | bytes 2555912 | tf_op jit(solution)/shard_map/cond/branch_0_fun/ppermute | solution.py:37
  61.9 34.1 %collective-permute-start.24 = (bf16[416,1024]{1,0:T(8,128)(2,1)S(1)}, bf16[416,1024]{1,0:T(8,128)(2,1)}, u32[]{:S(2)}, u32[]{:S(2)}) collective-permute-start(bf16[416,1024]{1,0:T(8,128)(2,1)S(1)} %get-tuple-element.65), channel_id=1, source_target_pairs={{8,16},{16,8},{9,17},{17,9},{10,18},{18,10},{11,19},{19,11},{12,20... | collective-permute-start | bytes 2555912 | tf_op jit(solution)/shard_map/cond/branch_0_fun/ppermute | solution.py:41
  64.9 32.9 %collective-permute-start.19 = (bf16[416,1024]{1,0:T(8,128)(2,1)}, bf16[416,1024]{1,0:T(8,128)(2,1)}, u32[]{:S(2)}, u32[]{:S(2)}) collective-permute-start(bf16[416,1024]{1,0:T(8,128)(2,1)} %collective-permute-done.15), channel_id=1, source_target_pairs={{0,6},{1,7},{2,4},{3,5},{4,2},{5,3},{6,0},{7,1},{8,14},{9,15},{10,... | collective-permute-start | bytes 2555912 | tf_op jit(solution)/shard_map/cond/branch_0_fun/ppermute | solution.py:49
  73.9 31.8 %collective-permute-start.17 = (bf16[416,1024]{1,0:T(8,128)(2,1)}, bf16[416,1024]{1,0:T(8,128)(2,1)S(1)}, u32[]{:S(2)}, u32[]{:S(2)}) collective-permute-start(bf16[416,1024]{1,0:T(8,128)(2,1)} %copy-done.95), channel_id=1, source_target_pairs={{0,1},{1,0},{2,3},{3,2},{4,5},{5,4},{6,7},{7,6},{8,9},{9,8},{10,11... | collective-permute-start | bytes 2555912 | tf_op jit(solution)/shard_map/cond/branch_0_fun/ppermute | solution.py:49
  76.2 32.1 %collective-permute-start.10 = (bf16[416,1024]{1,0:T(8,128)(2,1)}, bf16[416,1024]{1,0:T(8,128)(2,1)S(1)}, u32[]{:S(2)}, u32[]{:S(2)}) collective-permute-start(bf16[416,1024]{1,0:T(8,128)(2,1)} %copy-done.89), channel_id=1, source_target_pairs={{8,16},{16,8},{9,17},{17,9},{10,18},{18,10},{11,19},{19,11},{12,20... | collective-permute-start | bytes 2555912 | tf_op jit(solution)/shard_map/cond/branch_0_fun/ppermute | solution.py:41
  91.5 21.1 %collective-permute-start.11 = (bf16[416,1024]{1,0:T(8,128)(2,1)S(1)}, bf16[416,1024]{1,0:T(8,128)(2,1)S(1)}, u32[]{:S(2)}, u32[]{:S(2)}) collective-permute-start(bf16[416,1024]{1,0:T(8,128)(2,1)S(1)} %copy-done.72), channel_id=1, source_target_pairs={{0,6},{1,7},{2,4},{3,5},{4,2},{5,3},{6,0},{7,1},{8,14},{9,15},{10,... | collective-permute-start | bytes 2555912 | tf_op jit(solution)/shard_map/cond/branch_0_fun/ppermute | solution.py:49
  96.0 17.4 %collective-permute-start.30 = (bf16[416,1024]{1,0:T(8,128)(2,1)}, bf16[416,1024]{1,0:T(8,128)(2,1)S(1)}, u32[]{:S(2)}, u32[]{:S(2)}) collective-permute-start(bf16[416,1024]{1,0:T(8,128)(2,1)} %collective-permute-done.27), channel_id=1, source_target_pairs={{8,16},{16,8},{9,17},{17,9},{10,18},{18,10},{11,19},{19,11},{12,20... | collective-permute-start | bytes 2555912 | tf_op jit(solution)/shard_map/cond/branch_0_fun/ppermute | solution.py:41
  97.8 26.0 %collective-permute-start.16 = (bf16[416,1024]{1,0:T(8,128)(2,1)}, bf16[416,1024]{1,0:T(8,128)(2,1)S(1)}, u32[]{:S(2)}, u32[]{:S(2)}) collective-permute-start(bf16[416,1024]{1,0:T(8,128)(2,1)} %collective-permute-done.15), channel_id=1, source_target_pairs={{0,8},{24,16},{1,9},{25,17},{2,10},{26,18},{3,11},{27,19},{4,12},{... | collective-permute-start | bytes 2555912 | tf_op jit(solution)/shard_map/cond/branch_0_fun/ppermute | solution.py:37
  105.7 34.0 %collective-permute-start.1 = (bf16[416,1024]{1,0:T(8,128)(2,1)S(1)}, bf16[416,1024]{1,0:T(8,128)(2,1)S(1)}, u32[]{:S(2)}, u32[]{:S(2)}) collective-permute-start(bf16[416,1024]{1,0:T(8,128)(2,1)S(1)} %copy-done.72), channel_id=1, source_target_pairs={{0,8},{24,16},{1,9},{25,17},{2,10},{26,18},{3,11},{27,19},{4,12},{... | collective-permute-start | bytes 2555912 | tf_op jit(solution)/shard_map/cond/branch_0_fun/ppermute | solution.py:37
  108.3 35.9 %collective-permute-start.3 = (bf16[416,1024]{1,0:T(8,128)(2,1)}, bf16[416,1024]{1,0:T(8,128)(2,1)S(1)}, u32[]{:S(2)}, u32[]{:S(2)}) collective-permute-start(bf16[416,1024]{1,0:T(8,128)(2,1)} %collective-permute-done.2), channel_id=1, source_target_pairs={{0,1},{1,0},{2,3},{3,2},{4,5},{5,4},{6,7},{7,6},{8,9},{9,8},{10,11... | collective-permute-start | bytes 2555912 | tf_op jit(solution)/shard_map/cond/branch_0_fun/ppermute | solution.py:49
  112.6 32.3 %collective-permute-start.5 = (bf16[416,1024]{1,0:T(8,128)(2,1)S(1)}, bf16[416,1024]{1,0:T(8,128)(2,1)S(1)}, u32[]{:S(2)}, u32[]{:S(2)}) collective-permute-start(bf16[416,1024]{1,0:T(8,128)(2,1)S(1)} %copy-done.60), channel_id=1, source_target_pairs={{8,16},{16,8},{9,17},{17,9},{10,18},{18,10},{11,19},{19,11},{12,20... | collective-permute-start | bytes 2555912 | tf_op jit(solution)/shard_map/cond/branch_0_fun/ppermute | solution.py:41
  113.4 35.1 %collective-permute-start.25 = (bf16[416,1024]{1,0:T(8,128)(2,1)}, bf16[416,1024]{1,0:T(8,128)(2,1)S(1)}, u32[]{:S(2)}, u32[]{:S(2)}) collective-permute-start(bf16[416,1024]{1,0:T(8,128)(2,1)} %collective-permute-done.7), channel_id=1, source_target_pairs={{8,16},{16,8},{9,17},{17,9},{10,18},{18,10},{11,19},{19,11},{12,20... | collective-permute-start | bytes 2555912 | tf_op jit(solution)/shard_map/cond/branch_0_fun/ppermute | solution.py:41
  123.8 24.8 %collective-permute-start.18 = (bf16[416,1024]{1,0:T(8,128)(2,1)S(1)}, bf16[416,1024]{1,0:T(8,128)(2,1)S(1)}, u32[]{:S(2)}, u32[]{:S(2)}) collective-permute-start(bf16[416,1024]{1,0:T(8,128)(2,1)S(1)} %collective-permute-done.10), channel_id=1, source_target_pairs={{0,1},{1,0},{2,3},{3,2},{4,5},{5,4},{6,7},{7,6},{8,9},{9,8},{10,11... | collective-permute-start | bytes 2555912 | tf_op jit(solution)/shard_map/cond/branch_0_fun/ppermute | solution.py:49
  139.7 27.8 %collective-permute-start.20 = (bf16[416,1024]{1,0:T(8,128)(2,1)}, bf16[416,1024]{1,0:T(8,128)(2,1)S(1)}, u32[]{:S(2)}, u32[]{:S(2)}) collective-permute-start(bf16[416,1024]{1,0:T(8,128)(2,1)} %collective-permute-done.19), channel_id=1, source_target_pairs={{0,8},{24,16},{1,9},{25,17},{2,10},{26,18},{3,11},{27,19},{4,12},{... | collective-permute-start | bytes 2555912 | tf_op jit(solution)/shard_map/cond/branch_0_fun/ppermute | solution.py:37
  144.3 25.8 %collective-permute-start.21 = (bf16[416,1024]{1,0:T(8,128)(2,1)S(1)}, bf16[416,1024]{1,0:T(8,128)(2,1)S(1)}, u32[]{:S(2)}, u32[]{:S(2)}) collective-permute-start(bf16[416,1024]{1,0:T(8,128)(2,1)S(1)} %collective-permute-done.17), channel_id=1, source_target_pairs={{0,6},{1,7},{2,4},{3,5},{4,2},{5,3},{6,0},{7,1},{8,14},{9,15},{10,... | collective-permute-start | bytes 2555912 | tf_op jit(solution)/shard_map/cond/branch_0_fun/ppermute | solution.py:49
  144.9 33.9 %collective-permute-start.12 = (bf16[416,1024]{1,0:T(8,128)(2,1)S(1)}, bf16[416,1024]{1,0:T(8,128)(2,1)S(1)}, u32[]{:S(2)}, u32[]{:S(2)}) collective-permute-start(bf16[416,1024]{1,0:T(8,128)(2,1)S(1)} %collective-permute-done.11), channel_id=1, source_target_pairs={{0,8},{24,16},{1,9},{25,17},{2,10},{26,18},{3,11},{27,19},{4,12},{... | collective-permute-start | bytes 2555912 | tf_op jit(solution)/shard_map/cond/branch_0_fun/ppermute | solution.py:37
  148.5 4.7 %collective-permute-start.6 = (bf16[416,1024]{1,0:T(8,128)(2,1)S(1)}, bf16[416,1024]{1,0:T(8,128)(2,1)}, u32[]{:S(2)}, u32[]{:S(2)}) collective-permute-start(bf16[416,1024]{1,0:T(8,128)(2,1)S(1)} %collective-permute-done.5), channel_id=1, source_target_pairs={{0,1},{1,0},{2,3},{3,2},{4,5},{5,4},{6,7},{7,6},{8,9},{9,8},{10,11... | collective-permute-start | bytes 2555912 | tf_op jit(solution)/shard_map/cond/branch_0_fun/ppermute | solution.py:49
  148.7 36.7 %collective-permute-start.13 = (bf16[416,1024]{1,0:T(8,128)(2,1)S(1)}, bf16[416,1024]{1,0:T(8,128)(2,1)S(1)}, u32[]{:S(2)}, u32[]{:S(2)}) collective-permute-start(bf16[416,1024]{1,0:T(8,128)(2,1)S(1)} %collective-permute-done.3), channel_id=1, source_target_pairs={{0,6},{1,7},{2,4},{3,5},{4,2},{5,3},{6,0},{7,1},{8,14},{9,15},{10,... | collective-permute-start | bytes 2555912 | tf_op jit(solution)/shard_map/cond/branch_0_fun/ppermute | solution.py:49
  164.1 39.5 %collective-permute-start.22 = (bf16[416,1024]{1,0:T(8,128)(2,1)S(1)}, bf16[416,1024]{1,0:T(8,128)(2,1)S(1)}, u32[]{:S(2)}, u32[]{:S(2)}) collective-permute-start(bf16[416,1024]{1,0:T(8,128)(2,1)S(1)} %collective-permute-done.18), channel_id=1, source_target_pairs={{0,6},{1,7},{2,4},{3,5},{4,2},{5,3},{6,0},{7,1},{8,14},{9,15},{10,... | collective-permute-start | bytes 2555912 | tf_op jit(solution)/shard_map/cond/branch_0_fun/ppermute | solution.py:49
  167.5 51.0 %collective-permute-start.14 = (bf16[416,1024]{1,0:T(8,128)(2,1)}, bf16[416,1024]{1,0:T(8,128)(2,1)}, u32[]{:S(2)}, u32[]{:S(2)}) collective-permute-start(bf16[416,1024]{1,0:T(8,128)(2,1)} %collective-permute-done.6), channel_id=1, source_target_pairs={{0,6},{1,7},{2,4},{3,5},{4,2},{5,3},{6,0},{7,1},{8,14},{9,15},{10,... | collective-permute-start | bytes 2555912 | tf_op jit(solution)/shard_map/cond/branch_0_fun/ppermute | solution.py:49
  251.7 23.7 %collective-permute-start.31 = (f16[848,416]{0,1:T(8,128)(2,1)}, f16[848,416]{0,1:T(8,128)(2,1)}, u32[]{:S(2)}, u32[]{:S(2)}) collective-permute-start(f16[848,416]{0,1:T(8,128)(2,1)} %concatenate.157), channel_id=1, source_target_pairs={{8,0},{16,24},{9,1},{17,25},{10,2},{18,26},{11,3},{19,27},{12,4},{... | collective-permute-start | bytes 2116616 | tf_op jit(solution)/shard_map/cond/branch_0_fun/ppermute | solution.py:45
  259.1 31.9 %collective-permute-start.28 = (f16[848,416]{0,1:T(8,128)(2,1)}, f16[848,416]{0,1:T(8,128)(2,1)}, u32[]{:S(2)}, u32[]{:S(2)}) collective-permute-start(f16[848,416]{0,1:T(8,128)(2,1)} %concatenate.155), channel_id=1, source_target_pairs={{8,0},{16,24},{9,1},{17,25},{10,2},{18,26},{11,3},{19,27},{12,4},{... | collective-permute-start | bytes 2116616 | tf_op jit(solution)/shard_map/cond/branch_0_fun/ppermute | solution.py:45
  264.5 42.4 %collective-permute-start.26 = (f16[848,416]{0,1:T(8,128)(2,1)}, f16[848,416]{0,1:T(8,128)(2,1)}, u32[]{:S(2)}, u32[]{:S(2)}) collective-permute-start(f16[848,416]{0,1:T(8,128)(2,1)} %concatenate.153), channel_id=1, source_target_pairs={{8,0},{16,24},{9,1},{17,25},{10,2},{18,26},{11,3},{19,27},{12,4},{... | collective-permute-start | bytes 2116616 | tf_op jit(solution)/shard_map/cond/branch_0_fun/ppermute | solution.py:45
  268.2 53.8 %collective-permute-start.23 = (f16[848,416]{0,1:T(8,128)(2,1)}, f16[848,416]{0,1:T(8,128)(2,1)}, u32[]{:S(2)}, u32[]{:S(2)}) collective-permute-start(f16[848,416]{0,1:T(8,128)(2,1)} %concatenate.151), channel_id=1, source_target_pairs={{8,0},{16,24},{9,1},{17,25},{10,2},{18,26},{11,3},{19,27},{12,4},{... | collective-permute-start | bytes 2116616 | tf_op jit(solution)/shard_map/cond/branch_0_fun/ppermute | solution.py:45
  (41 other events, 516.5 us)
